TPU v7x, 256 devices: a whole 4x4x8 slice. The times are simulated.
256 devices in a mesh: tm: 256 (over x, y, z, core).
Axes of the slice: x: 4, y: 4, z: 8, core: 2. Of those that a mesh axis runs over, the one named last changes fastest.
Arguments:
- samples: float32 [256, 2, 256, 256], P('tm'), may hold values from -0.5 to 0.5
Outputs:
- propagators: float32 [256, 2, 256, 256], P('tm')
All inputs are finite; a program needn't handle non-finite values.
Results may differ from a plain program's by a relative error of at most 0.0003.
Values sent between devices are 32-bit elements; how exact they have to be, the bound alone decides.
A program may use at most 64 MiB of HBM per device.

v0:
```python
import jax
import jax.numpy as jnp
from jax import lax
from jax.sharding import PartitionSpec as P

time_step = 0.25


def shifted(x, axis, by):
    size = lax.axis_size(axis)
    return lax.ppermute(x, axis, [(i, (i + by) % size) for i in range(size)])


def from_behind(x, axis, by):
    size = lax.axis_size(axis)
    pairs = [(i, i + by) for i in range(size) if 0 <= i + by < size]
    return lax.ppermute(x, axis, pairs)


def complex_product(left, right):
    size = left.shape[-1]
    joined = jnp.concatenate([right[0], right[1]], axis=1)
    real_rows = jnp.dot(
        left[0], joined, preferred_element_type=jnp.float32, precision=lax.Precision.HIGHEST
    )
    imag_rows = jnp.dot(
        left[1], joined, preferred_element_type=jnp.float32, precision=lax.Precision.HIGHEST
    )
    real_part = real_rows[:, :size] - imag_rows[:, size:]
    imag_part = real_rows[:, size:] + imag_rows[:, :size]
    return jnp.stack([real_part, imag_part])


def hermitian(drawn):
    return jnp.stack([(drawn[0] + drawn[0].T) * 0.5, (drawn[1] - drawn[1].T) * 0.5])


def unit_matrix(size):
    return jnp.stack([jnp.eye(size, dtype=jnp.float32), jnp.zeros((size, size), jnp.float32)])


def magnus_factor(first, second):
    size = first.shape[-1]
    summed = first + second
    product = complex_product(second, first)
    comm_real = product[0] - product[0].T
    comm_imag = product[1] + product[1].T
    shrink = time_step * time_step / 12.0
    omega = jnp.stack(
        [
            0.5 * time_step * summed[1] - shrink * comm_real,
            -0.5 * time_step * summed[0] - shrink * comm_imag,
        ]
    )
    identity = unit_matrix(size)
    nested = identity + omega / 4.0
    nested = identity + complex_product(omega, nested) / 3.0
    nested = identity + complex_product(omega, nested) / 2.0
    return identity + complex_product(omega, nested)


def on_device(samples):
    current = hermitian(samples[0])
    following = shifted(current, "tm", -1)
    factor = magnus_factor(current, following)
    cumulative = factor
    position = lax.axis_index("tm")
    devices = lax.axis_size("tm")
    stride = 1
    while stride < devices:
        received = from_behind(cumulative, "tm", stride)
        cumulative = jnp.where(
            position >= stride, complex_product(cumulative, received), cumulative
        )
        stride = stride * 2
    return cumulative[None]


def solution(mesh):
    in_specs = (P("tm", None, None, None),)
    out_specs = P("tm", None, None, None)
    return jax.shard_map(
        on_device, mesh=mesh, in_specs=in_specs, out_specs=out_specs, check_vma=False
    )
```

profile of v0, /device:TPU:102, one launch (start us, length us, event | category | flops | bytes accessed | tf_op | source)
XLA Modules:
  0.0 206.7 jit_solution(8241383880573714400)
XLA Ops:
  2.4 6.7 %collective-permute-done = f32[2,256,256]{2,1,0:T(8,128)S(1)} collective-permute-done((f32[2,256,256]{2,1,0:T(8,128)S(1)}, f32[2,256,256]{2,1,0:T(8,128)S(1)}, u32[]{:S(2)}, u32[]{:S(2)}) %collective-permute-start) | collective-permute-done | bytes 524320 | tf_op jit(solution)/shard_map/ppermute | solution.py:11
  15.4 5.3 %collective-permute-start.1 = (f32[2,256,256]{2,1,0:T(8,128)S(1)}, f32[2,256,256]{2,1,0:T(8,128)S(1)}, u32[]{:S(2)}, u32[]{:S(2)}) collective-permute-start(f32[2,256,256]{2,1,0:T(8,128)S(1)} %convert_add_fusion), channel_id=1, source_target_pairs={{0,1},{1,2},{2,3},{3,4},{4,5},{5,6},{6,7},{7,8},{8,9},{9,10},{10,1... | collective-permute-start | bytes 1572872 | tf_op jit(solution)/shard_map/ppermute | solution.py:17
  20.7 5.3 %collective-permute-done.1 = f32[2,256,256]{2,1,0:T(8,128)S(1)} collective-permute-done((f32[2,256,256]{2,1,0:T(8,128)S(1)}, f32[2,256,256]{2,1,0:T(8,128)S(1)}, u32[]{:S(2)}, u32[]{:S(2)}) %collective-permute-start.1) | collective-permute-done | bytes 524320 | tf_op jit(solution)/shard_map/ppermute | solution.py:17
  27.5 6.3 %collective-permute-start.2 = (f32[2,256,256]{2,1,0:T(8,128)S(1)}, f32[2,256,256]{2,1,0:T(8,128)S(1)}, u32[]{:S(2)}, u32[]{:S(2)}) collective-permute-start(f32[2,256,256]{2,1,0:T(8,128)S(1)} %maximum_select_fusion), channel_id=1, source_target_pairs={{0,2},{1,3},{2,4},{3,5},{4,6},{5,7},{6,8},{7,9},{8,10},{9,11},{10,... | collective-permute-start | bytes 1572872 | tf_op jit(solution)/shard_map/ppermute | solution.py:17
  33.8 10.2 %collective-permute-done.2 = f32[2,256,256]{2,1,0:T(8,128)S(1)} collective-permute-done((f32[2,256,256]{2,1,0:T(8,128)S(1)}, f32[2,256,256]{2,1,0:T(8,128)S(1)}, u32[]{:S(2)}, u32[]{:S(2)}) %collective-permute-start.2) | collective-permute-done | bytes 524320 | tf_op jit(solution)/shard_map/ppermute | solution.py:17
  45.5 3.8 %collective-permute-start.3 = (f32[2,256,256]{2,1,0:T(8,128)S(1)}, f32[2,256,256]{2,1,0:T(8,128)S(1)}, u32[]{:S(2)}, u32[]{:S(2)}) collective-permute-start(f32[2,256,256]{2,1,0:T(8,128)S(1)} %maximum_select_fusion.1), channel_id=1, source_target_pairs={{0,4},{1,5},{2,6},{3,7},{4,8},{5,9},{6,10},{7,11},{8,12},{9,13},{1... | collective-permute-start | bytes 1572872 | tf_op jit(solution)/shard_map/ppermute | solution.py:17
  49.3 22.8 %collective-permute-done.3 = f32[2,256,256]{2,1,0:T(8,128)S(1)} collective-permute-done((f32[2,256,256]{2,1,0:T(8,128)S(1)}, f32[2,256,256]{2,1,0:T(8,128)S(1)}, u32[]{:S(2)}, u32[]{:S(2)}) %collective-permute-start.3) | collective-permute-done | bytes 524320 | tf_op jit(solution)/shard_map/ppermute | solution.py:17
  73.7 29.6 %collective-permute-start.4 = (f32[2,256,256]{2,1,0:T(8,128)S(1)}, f32[2,256,256]{2,1,0:T(8,128)S(1)}, u32[]{:S(2)}, u32[]{:S(2)}) collective-permute-start(f32[2,256,256]{2,1,0:T(8,128)S(1)} %maximum_select_fusion.2), channel_id=1, source_target_pairs={{0,8},{1,9},{2,10},{3,11},{4,12},{5,13},{6,14},{7,15},{8,16},{9,17... | collective-permute-start | bytes 1572872 | tf_op jit(solution)/shard_map/ppermute | solution.py:17
  103.3 14.6 %collective-permute-done.4 = f32[2,256,256]{2,1,0:T(8,128)S(1)} collective-permute-done((f32[2,256,256]{2,1,0:T(8,128)S(1)}, f32[2,256,256]{2,1,0:T(8,128)S(1)}, u32[]{:S(2)}, u32[]{:S(2)}) %collective-permute-start.4) | collective-permute-done | bytes 524320 | tf_op jit(solution)/shard_map/ppermute | solution.py:17
  119.4 6.0 %collective-permute-start.5 = (f32[2,256,256]{2,1,0:T(8,128)S(1)}, f32[2,256,256]{2,1,0:T(8,128)}, u32[]{:S(2)}, u32[]{:S(2)}) collective-permute-start(f32[2,256,256]{2,1,0:T(8,128)S(1)} %maximum_select_fusion.3), channel_id=1, source_target_pairs={{0,16},{1,17},{2,18},{3,19},{4,20},{5,21},{6,22},{7,23},{8,24},{9,... | collective-permute-start | bytes 1572872 | tf_op jit(solution)/shard_map/ppermute | solution.py:17
  125.4 14.0 %collective-permute-done.5 = f32[2,256,256]{2,1,0:T(8,128)} collective-permute-done((f32[2,256,256]{2,1,0:T(8,128)S(1)}, f32[2,256,256]{2,1,0:T(8,128)}, u32[]{:S(2)}, u32[]{:S(2)}) %collective-permute-start.5) | collective-permute-done | bytes 524320 | tf_op jit(solution)/shard_map/ppermute | solution.py:17
  142.8 3.3 %collective-permute-start.6 = (f32[2,256,256]{2,1,0:T(8,128)}, f32[2,256,256]{2,1,0:T(8,128)}, u32[]{:S(2)}, u32[]{:S(2)}) collective-permute-start(f32[2,256,256]{2,1,0:T(8,128)} %maximum_select_fusion.4), channel_id=1, source_target_pairs={{0,32},{1,33},{2,34},{3,35},{4,36},{5,37},{6,38},{7,39},{8,40},{9,... | collective-permute-start | bytes 1572872 | tf_op jit(solution)/shard_map/ppermute | solution.py:17
  146.1 13.9 %collective-permute-done.6 = f32[2,256,256]{2,1,0:T(8,128)} collective-permute-done((f32[2,256,256]{2,1,0:T(8,128)}, f32[2,256,256]{2,1,0:T(8,128)}, u32[]{:S(2)}, u32[]{:S(2)}) %collective-permute-start.6) | collective-permute-done | bytes 524320 | tf_op jit(solution)/shard_map/ppermute | solution.py:17
  161.1 1.6 fusion.5
  162.7 1.6 fusion.6
  165.4 1.3 collective-permute-start.7
  166.7 12.6 %collective-permute-done.7 = f32[2,256,256]{2,1,0:T(8,128)} collective-permute-done((f32[2,256,256]{2,1,0:T(8,128)}, f32[2,256,256]{2,1,0:T(8,128)}, u32[]{:S(2)}, u32[]{:S(2)}) %collective-permute-start.7) | collective-permute-done | bytes 524320 | tf_op jit(solution)/shard_map/ppermute | solution.py:17
  180.4 1.6 fusion.3
  182.0 1.6 fusion.4
  185.7 1.3 collective-permute-start.8
  187.0 13.2 %collective-permute-done.8 = f32[2,256,256]{2,1,0:T(8,128)} collective-permute-done((f32[2,256,256]{2,1,0:T(8,128)}, f32[2,256,256]{2,1,0:T(8,128)}, u32[]{:S(2)}, u32[]{:S(2)}) %collective-permute-start.8) | collective-permute-done | bytes 524320 | tf_op jit(solution)/shard_map/ppermute | solution.py:17
  201.3 1.6 fusion.1
  202.8 1.6 fusion.2
  205.5 1.2 fusion
  (82 shorter events, 25.1 us)
Async XLA Ops:
  1.1 1.0 copy-start.7
  2.2 6.8 %collective-permute-start = (f32[2,256,256]{2,1,0:T(8,128)S(1)}, f32[2,256,256]{2,1,0:T(8,128)S(1)}, u32[]{:S(2)}, u32[]{:S(2)}) collective-permute-start(f32[2,256,256]{2,1,0:T(8,128)S(1)} %pad_maximum_fusion), channel_id=1, source_target_pairs={{0,255},{1,0},{2,1},{3,2},{4,3},{5,4},{6,5},{7,6},{8,7},{9,8},{10,... | collective-permute-start | bytes 1572872 | tf_op jit(solution)/shard_map/ppermute | solution.py:11
  15.4 10.7 %collective-permute-start.1 = (f32[2,256,256]{2,1,0:T(8,128)S(1)}, f32[2,256,256]{2,1,0:T(8,128)S(1)}, u32[]{:S(2)}, u32[]{:S(2)}) collective-permute-start(f32[2,256,256]{2,1,0:T(8,128)S(1)} %convert_add_fusion), channel_id=1, source_target_pairs={{0,1},{1,2},{2,3},{3,4},{4,5},{5,6},{6,7},{7,8},{8,9},{9,10},{10,1... | collective-permute-start | bytes 1572872 | tf_op jit(solution)/shard_map/ppermute | solution.py:17
  27.5 16.5 %collective-permute-start.2 = (f32[2,256,256]{2,1,0:T(8,128)S(1)}, f32[2,256,256]{2,1,0:T(8,128)S(1)}, u32[]{:S(2)}, u32[]{:S(2)}) collective-permute-start(f32[2,256,256]{2,1,0:T(8,128)S(1)} %maximum_select_fusion), channel_id=1, source_target_pairs={{0,2},{1,3},{2,4},{3,5},{4,6},{5,7},{6,8},{7,9},{8,10},{9,11},{10,... | collective-permute-start | bytes 1572872 | tf_op jit(solution)/shard_map/ppermute | solution.py:17
  45.5 26.7 %collective-permute-start.3 = (f32[2,256,256]{2,1,0:T(8,128)S(1)}, f32[2,256,256]{2,1,0:T(8,128)S(1)}, u32[]{:S(2)}, u32[]{:S(2)}) collective-permute-start(f32[2,256,256]{2,1,0:T(8,128)S(1)} %maximum_select_fusion.1), channel_id=1, source_target_pairs={{0,4},{1,5},{2,6},{3,7},{4,8},{5,9},{6,10},{7,11},{8,12},{9,13},{1... | collective-permute-start | bytes 1572872 | tf_op jit(solution)/shard_map/ppermute | solution.py:17
  73.7 44.2 %collective-permute-start.4 = (f32[2,256,256]{2,1,0:T(8,128)S(1)}, f32[2,256,256]{2,1,0:T(8,128)S(1)}, u32[]{:S(2)}, u32[]{:S(2)}) collective-permute-start(f32[2,256,256]{2,1,0:T(8,128)S(1)} %maximum_select_fusion.2), channel_id=1, source_target_pairs={{0,8},{1,9},{2,10},{3,11},{4,12},{5,13},{6,14},{7,15},{8,16},{9,17... | collective-permute-start | bytes 1572872 | tf_op jit(solution)/shard_map/ppermute | solution.py:17
  119.4 20.0 %collective-permute-start.5 = (f32[2,256,256]{2,1,0:T(8,128)S(1)}, f32[2,256,256]{2,1,0:T(8,128)}, u32[]{:S(2)}, u32[]{:S(2)}) collective-permute-start(f32[2,256,256]{2,1,0:T(8,128)S(1)} %maximum_select_fusion.3), channel_id=1, source_target_pairs={{0,16},{1,17},{2,18},{3,19},{4,20},{5,21},{6,22},{7,23},{8,24},{9,... | collective-permute-start | bytes 1572872 | tf_op jit(solution)/shard_map/ppermute | solution.py:17
  142.8 17.2 %collective-permute-start.6 = (f32[2,256,256]{2,1,0:T(8,128)}, f32[2,256,256]{2,1,0:T(8,128)}, u32[]{:S(2)}, u32[]{:S(2)}) collective-permute-start(f32[2,256,256]{2,1,0:T(8,128)} %maximum_select_fusion.4), channel_id=1, source_target_pairs={{0,32},{1,33},{2,34},{3,35},{4,36},{5,37},{6,38},{7,39},{8,40},{9,... | collective-permute-start | bytes 1572872 | tf_op jit(solution)/shard_map/ppermute | solution.py:17
  164.4 1.1 copy-start
  165.4 13.9 %collective-permute-start.7 = (f32[2,256,256]{2,1,0:T(8,128)}, f32[2,256,256]{2,1,0:T(8,128)}, u32[]{:S(2)}, u32[]{:S(2)}) collective-permute-start(f32[2,256,256]{2,1,0:T(8,128)} %maximum_select_fusion.5), channel_id=1, source_target_pairs={{0,64},{1,65},{2,66},{3,67},{4,68},{5,69},{6,70},{7,71},{8,72},{9,... | collective-permute-start | bytes 1572872 | tf_op jit(solution)/shard_map/ppermute | solution.py:17
  183.6 1.0 copy-start.1
  183.6 2.0 copy-start.3
  183.6 2.0 copy-start.5
  185.7 14.5 %collective-permute-start.8 = (f32[2,256,256]{2,1,0:T(8,128)}, f32[2,256,256]{2,1,0:T(8,128)}, u32[]{:S(2)}, u32[]{:S(2)}) collective-permute-start(f32[2,256,256]{2,1,0:T(8,128)} %maximum_select_fusion.6), channel_id=1, source_target_pairs={{0,128},{1,129},{2,130},{3,131},{4,132},{5,133},{6,134},{7,135},{8... | collective-permute-start | bytes 1572872 | tf_op jit(solution)/shard_map/ppermute | solution.py:17
  204.4 1.0 copy-start.2
  204.4 1.0 copy-start.4
  204.4 1.1 copy-start.6
where the time goes:
time: 207 us
  waiting for transfers between devices  114 us (55%)
  starting transfers between devices  56.9 us (27%)
  matrix products  20.4 us (10%)
  local copies, waits for them, and re-layouts  8.97 us (4%)
  other arithmetic  6.28 us (3%)
    ppermute x8, waiting for transfers between devices, from_behind(): return lax.ppermute(x, axis, pairs)  107 us
    ppermute x8, starting transfers between devices, from_behind(): return lax.ppermute(x, axis, pairs)  56.8 us
    dot_general x12, matrix products, complex_product(): jnp.dot(left[1], joined, preferred_element_type=jnp.float32, precision=la...  10.2 us
    dot_general x12, matrix products, complex_product(): jnp.dot(left[0], joined, preferred_element_type=jnp.float32, precision=la...  10.2 us
    ppermute x1, waiting for transfers between devices, shifted(): return lax.ppermute(x, axis, [(i, (i + by) % size) for i in range(size)])  6.66 us
    squeeze x11, local copies, waits for them, and re-layouts, complex_product(): joined = jnp.concatenate([right[0], right[1]], axis=1)  4.5 us
  transfers between devices with their start and end apart: 9, of which 9 were waited for; matrix products, arithmetic and copies ran while one was open for 0% of the time, Pallas kernels for 0%

commit v1 on v0

v1 whole, which is shorter than its diff:
```python
import functools

import jax
import jax.numpy as jnp
from jax import lax
from jax.experimental import pallas as pl
from jax.experimental.pallas import tpu as pltpu
from jax.sharding import PartitionSpec as P

MESH = pl.DeviceIdType.MESH
time_step = 0.25
SLABS = 4


def halves(x):
    high = x.astype(jnp.bfloat16)
    return high, (x - high.astype(jnp.float32)).astype(jnp.bfloat16)


def dot(a, b):
    return jnp.dot(a, b, preferred_element_type=jnp.float32)


def product(x, high, low):
    m = x.shape[0]
    xh, xl = halves(x)
    both = jnp.concatenate([xh, xl], axis=0)
    by_real = dot(both, high[0])
    by_imag = dot(both, high[1])
    by_real = by_real[:m] + by_real[m:] + dot(xh, low[0])
    by_imag = by_imag[:m] + by_imag[m:] + dot(xh, low[1])
    n = m // 2
    return by_real[:n] - by_imag[n:], by_imag[:n] + by_real[n:]


def each_slab(body):
    lax.fori_loop(0, SLABS, body, 0)


def kernel(
    devices, x_ref, o_ref,
    packed, packed_in, value, unit, keep, got, swap, last, high, low,
    h_send, h_recv, u_send, u_recv, g_send, g_recv, s_send, s_recv, f_send, f_recv,
):
    size = x_ref.shape[-1]
    width = size // (2 * SLABS)
    chips = devices // 2
    me = lax.axis_index("tm")
    core = lax.rem(me, 2)
    chip = me // 2
    other = me + 1 - 2 * core
    before = lax.rem(me + devices - 1, devices)
    after = lax.rem(me + 1, devices)

    stages = []
    shift = 1
    while shift < chips:
        stages.append((shift, chip >= shift, chip + shift < chips))
        shift *= 2
    n_stages = len(stages)

    barrier = pltpu.get_barrier_semaphore()

    def greet(device):
        pl.semaphore_signal(barrier, inc=1, device_id=(device,), device_id_type=MESH)

    greet(other)
    greet(before)
    greet(after)
    expected = 3
    for shift, takes, gives in stages:
        pl.when(takes)(functools.partial(greet, me - 2 * shift))
        pl.when(gives)(functools.partial(greet, me + 2 * shift))
        expected = expected + takes.astype(jnp.int32) + gives.astype(jnp.int32)

    def remote(src, dst, send, recv, device):
        return pltpu.make_async_remote_copy(
            src_ref=src, dst_ref=dst, send_sem=send, recv_sem=recv,
            device_id=(device,), device_id_type=MESH,
        )

    row = lax.broadcasted_iota(jnp.int32, (size, size), 0)
    col = lax.broadcasted_iota(jnp.int32, (size, size), 1)
    h_real = (x_ref[0] + x_ref[0].T) * 0.5
    h_imag = (x_ref[1] - x_ref[1].T) * 0.5
    packed[...] = jnp.where(col >= row, h_real, h_imag)
    pl.semaphore_wait(barrier, expected)
    h_copy = remote(packed, packed_in, h_send, h_recv, before)
    h_copy.start()
    value[0] = h_real
    value[1] = h_imag
    for part, h in enumerate((h_real, h_imag)):
        high[0, 0, part], low[0, 0, part] = halves(h)
    h_copy.wait_recv()
    flat = packed_in[...]
    turned = flat.T
    n_real = jnp.where(col >= row, flat, turned)
    n_imag = jnp.where(row > col, flat, jnp.where(row < col, -turned, 0.0))
    x_real, x_imag = product(jnp.concatenate([n_real, n_imag], axis=0), high[0, 0], low[0, 0])
    shrink = time_step * time_step / 12.0
    m_real = shrink * (x_real - x_real.T) - 0.5 * time_step * (value[1] + n_imag)
    m_imag = -0.5 * time_step * (value[0] + n_real) - shrink * (x_imag + x_imag.T)
    for part, h in enumerate((m_real, m_imag)):
        high[0, 1, part], low[0, 1, part] = halves(h)
    eye = jnp.where(row == col, 1.0, 0.0)
    value[0] = eye + m_real * 0.25
    value[1] = m_imag * 0.25
    for divisor in (3.0, 2.0, 1.0):
        v_real, v_imag = product(
            jnp.concatenate([value[0], value[1]], axis=0), high[0, 1], low[0, 1]
        )
        if divisor == 1.0:
            value[0] = eye + v_real
            value[1] = v_imag
        else:
            value[0] = eye + v_real * (1.0 / divisor)
            value[1] = v_imag * (1.0 / divisor)
    for j in range(2 * SLABS):
        for part in range(2):
            unit[core, j, part] = value[part, j * width:(j + 1) * width]
    u_copy = remote(unit.at[core], unit.at[core], u_send, u_recv.at[core], other)
    u_copy.start()
    remote(unit.at[1 - core], unit.at[1 - core], u_send, u_recv.at[1 - core], other).wait_recv()

    for j in range(2 * SLABS):
        for part in range(2):
            rows = slice(j * width, (j + 1) * width)
            high[0, 0, part, rows], low[0, 0, part, rows] = halves(unit[1, j, part])
            high[1, 1, part, rows], low[1, 1, part, rows] = halves(unit[0, j, part])

    def give(s, j):
        shift = stages[s][0]
        return remote(keep.at[s, j, 0], got.at[s, j], g_send.at[s, j], g_recv.at[s, j], me + 2 * shift)

    def share(s, j, which):
        return remote(
            keep.at[s, j, which], swap.at[s, j, which],
            s_send.at[s, j, which], s_recv.at[s, j, which], other,
        )

    def finish(j):
        return remote(keep.at[n_stages, j, core], last.at[j], f_send.at[j], f_recv.at[j], other)

    def put(slot, which, first, part, value):
        rows = pl.ds(pl.multiple_of(first, width), width)
        high[slot, which, part, rows], low[slot, which, part, rows] = halves(value)

    def spread(s, j, which, real, imag):
        keep[s, j, which, 0] = real
        keep[s, j, which, 1] = imag
        if s < n_stages:
            first = core * (SLABS * width) + j * width
            put((s + 1) % 2, which, first, 0, real)
            put((s + 1) % 2, which, first, 1, imag)

    def chip_product(j, _):
        mine = core * SLABS + j
        x = unit[0, mine].reshape(2 * width, size)
        real, imag = product(x, high[0, 0], low[0, 0])
        spread(0, j, 0, real, imag)
        pl.when(stages[0][2])(lambda: give(0, j).start())
        share(0, j, 0).start()
        keep[0, j, 1] = unit[0, mine]
        return 0

    each_slab(chip_product)

    for s, (shift, takes, gives) in enumerate(stages):
        slot = (s + 1) % 2
        final = s + 1 == n_stages
        whichs = (0,) if s == 0 else (0, 1)

        def collect(j, _, s=s, slot=slot, whichs=whichs):
            for which in whichs:
                share(s, j, which).wait_recv()
                first = (1 - core) * (SLABS * width) + j * width
                put(slot, which, first, 0, swap[s, j, which, 0])
                put(slot, which, first, 1, swap[s, j, which, 1])
            return 0

        def take(j, _, s=s, slot=slot, final=final):
            give(s, j).wait_recv()
            x = got[s, j].reshape(2 * width, size)
            for which in (0, 1):
                real, imag = product(x, high[slot, which], low[slot, which])
                spread(s + 1, j, which, real, imag)
                if not final:
                    if which == 0:
                        pl.when(stages[s + 1][2])(lambda: give(s + 1, j).start())
                    share(s + 1, j, which).start()
            if final:
                finish(j).start()
            return 0

        def idle(j, _, s=s, final=final):
            keep[s + 1, j] = keep[s, j]
            if final:
                finish(j).start()
            else:
                pl.when(stages[s + 1][2])(lambda: give(s + 1, j).start())
            return 0

        if s == 0:
            each_slab(collect)
        else:
            pl.when(stages[s - 1][1])(functools.partial(each_slab, collect))
        pl.when(takes)(functools.partial(each_slab, take))
        pl.when(jnp.logical_not(takes))(functools.partial(each_slab, idle))

    def arrive(j, _):
        finish(j).wait_recv()
        for part in range(2):
            first = core * (SLABS * width) + j * width
            value[part, pl.ds(pl.multiple_of(first, width), width)] = keep[n_stages, j, 1 - core, part]
            first = (1 - core) * (SLABS * width) + j * width
            value[part, pl.ds(pl.multiple_of(first, width), width)] = last[j, part]
        return 0

    each_slab(arrive)
    o_ref[0] = value[0].T
    o_ref[1] = value[1].T

    h_copy.wait_send()
    u_copy.wait_send()

    def drain(j, _):
        for s, (shift, takes, gives) in enumerate(stages):
            pl.when(gives)(lambda s=s: give(s, j).wait_send())
            if s == 0:
                share(s, j, 0).wait_send()
            else:
                def both(s=s):
                    share(s, j, 0).wait_send()
                    share(s, j, 1).wait_send()
                pl.when(stages[s - 1][1])(both)
        finish(j).wait_send()
        return 0

    each_slab(drain)


def on_device(samples):
    x = samples[0]
    size = x.shape[-1]
    devices = lax.axis_size("tm")
    n_stages = (devices // 2).bit_length() - 1
    width = size // (2 * SLABS)
    f32, bf16 = jnp.float32, jnp.bfloat16
    slab = (2, width, size)
    dma = pltpu.SemaphoreType.DMA
    out = pl.pallas_call(
        functools.partial(kernel, devices),
        out_shape=jax.ShapeDtypeStruct(x.shape, f32),
        in_specs=[pl.BlockSpec(memory_space=pltpu.VMEM)],
        out_specs=pl.BlockSpec(memory_space=pltpu.VMEM),
        scratch_shapes=[
            pltpu.VMEM((size, size), f32),
            pltpu.VMEM((size, size), f32),
            pltpu.VMEM((2, size, size), f32),
            pltpu.VMEM((2, 2 * SLABS, *slab), f32),
            pltpu.VMEM((n_stages + 1, SLABS, 2, *slab), f32),
            pltpu.VMEM((n_stages, SLABS, *slab), f32),
            pltpu.VMEM((n_stages, SLABS, 2, *slab), f32),
            pltpu.VMEM((SLABS, *slab), f32),
            pltpu.VMEM((2, 2, 2, size, size), bf16),
            pltpu.VMEM((2, 2, 2, size, size), bf16),
            dma, dma, dma, dma((2,)),
            dma((n_stages, SLABS)), dma((n_stages, SLABS)),
            dma((n_stages, SLABS, 2)), dma((n_stages, SLABS, 2)),
            dma((SLABS,)), dma((SLABS,)),
        ],
        compiler_params=pltpu.CompilerParams(
            collective_id=0, has_side_effects=True, vmem_limit_bytes=48 << 20
        ),
        name="propagators",
    )(x)
    return out[None]


def solution(mesh):
    spec = P("tm", None, None, None)
    return jax.shard_map(on_device, mesh=mesh, in_specs=(spec,), out_specs=spec, check_vma=False)
```

time: 207 us -> 84.4 us (0.41)
  the two profiles are of different devices: /device:TPU:102 before, /device:TPU:61 now
where the time goes in v1:
time: 84.4 us; the launch traced here: 84.3 us
  Pallas kernels  82.5 us (98%)
  local copies, waits for them, and re-layouts  1.84 us (2%)
    pallas_call x1, Pallas kernels, on_device(): pl.pallas_call(functools.partial(kernel, devices), out_shape=jax.ShapeDty...  82.5 us
    unnamed x3, local copies, waits for them, and re-layouts  1.84 us

profile of v1, /device:TPU:61, one launch (start us, length us, event | category | flops | bytes accessed | tf_op | source)
XLA Modules:
  0.0 84.3 jit_solution(12145917800414814761)
XLA Ops:
  0.0 0.0 copy-start
  0.0 1.0 %copy-done = f32[1,2,256,256]{3,2,1,0:T(8,128)S(1)} copy-done((f32[1,2,256,256]{3,2,1,0:T(8,128)S(1)}, f32[1,2,256,256]{3,2,1,0:T(8,128)}, u32[]{:S(2)}) %copy-start) | copy-done | bytes 524312
  1.0 82.5 %propagators.1 = f32[2,256,256]{2,1,0:T(8,128)S(1)} custom-call(f32[2,256,256]{2,1,0:T(8,128)S(1)} %bitcast.3), custom_call_target="tpu_custom_call" | custom-call | tf_op jit(solution)/shard_map/propagators/pallas_call | solution.py:251
  83.5 0.8 copy.3
Async XLA Ops:
  0.0 1.0 %copy-start = (f32[1,2,256,256]{3,2,1,0:T(8,128)S(1)}, f32[1,2,256,256]{3,2,1,0:T(8,128)}, u32[]{:S(2)}) copy-start(f32[1,2,256,256]{3,2,1,0:T(8,128)} %param.1) | copy-start | bytes 1572868

commit v2 on v1

v2 whole, which is shorter than its diff:
```python
import functools

import jax
import jax.numpy as jnp
from jax import lax
from jax.experimental import pallas as pl
from jax.experimental.pallas import tpu as pltpu
from jax.sharding import PartitionSpec as P

MESH = pl.DeviceIdType.MESH
time_step = 0.25
WIDTH = 32
PARTS = 4


def halves(x):
    high = x.astype(jnp.bfloat16)
    return high, (x - high.astype(jnp.float32)).astype(jnp.bfloat16)


def dot(a, b):
    return jnp.dot(a, b, preferred_element_type=jnp.float32)


def product(x, high, low):
    m = x.shape[0]
    xh, xl = halves(x)
    both = jnp.concatenate([xh, xl], axis=0)
    by_real = dot(both, high[0])
    by_imag = dot(both, high[1])
    by_real = by_real[:m] + by_real[m:] + dot(xh, low[0])
    by_imag = by_imag[:m] + by_imag[m:] + dot(xh, low[1])
    n = m // 2
    return by_real[:n] - by_imag[n:], by_imag[:n] + by_real[n:]


def stacked(x):
    size = x.shape[-1]
    return jnp.concatenate([x[:, 0].reshape(-1, size), x[:, 1].reshape(-1, size)], axis=0)


def kernel(
    devices, x_ref, o_ref,
    drawn, packed, packed_in, value, unit, total, keep, got, swap, swap_second, last, crossed, high, low,
    x_sem, h_send, h_recv, u_send, u_recv, t_send, t_recv, p_send, p_recv, g_send, g_recv,
    s_send, s_recv, w_send, w_recv, f_send, f_recv, c_send, c_recv,
):
    size = x_ref.shape[-1]
    half = size // 2
    slabs = half // WIDTH
    per_part = slabs // PARTS
    chips = devices // 2
    me = lax.axis_index("tm")
    core = lax.rem(me, 2)
    chip = me // 2
    odd = lax.rem(chip, 2) == 1
    even = jnp.logical_not(odd)
    first_core = core == 0
    second_core = core == 1
    other = me + 1 - 2 * core
    before = lax.rem(me + devices - 1, devices)
    after = lax.rem(me + 1, devices)

    def device(chip, core):
        return chip * 2 + core

    shifts = []
    shift = 2
    while shift < chips:
        shifts.append(shift)
        shift *= 2
    n_shifts = len(shifts)
    takes = [odd] + [jnp.logical_and(odd, chip > by) for by in shifts]
    gives = [jnp.logical_and(odd, chip + by < chips) for by in shifts]
    gives_last = jnp.logical_and(odd, chip + 1 < chips)
    takes_last = jnp.logical_and(even, chip > 0)
    taken = sum(t.astype(jnp.int32) for t in takes)

    barrier = pltpu.get_barrier_semaphore()
    expected = 0

    def greet(when, device):
        @pl.when(when)
        def _():
            pl.semaphore_signal(barrier, inc=1, device_id=(device,), device_id_type=MESH)

        return when.astype(jnp.int32)

    always = chip >= 0
    pairs = [(always, other), (always, before), (always, after)]
    pairs += [(jnp.logical_and(even, second_core), device(chip + 1, c)) for c in range(2)]
    pairs += [(odd, device(chip - 1, 1))]
    for by, t, g in zip(shifts, takes[1:], gives):
        pairs += [(t, me - 2 * by), (g, me + 2 * by)]
    pairs += [(gives_last, me + 2), (takes_last, me - 2)]
    for when, where in pairs:
        expected = expected + greet(when, where)

    x_copy = pltpu.make_async_copy(x_ref, drawn, x_sem)
    x_copy.start()

    def remote(src, dst, send, recv, device):
        return pltpu.make_async_remote_copy(
            src_ref=src, dst_ref=dst, send_sem=send, recv_sem=recv,
            device_id=(device,), device_id_type=MESH,
        )

    row = lax.broadcasted_iota(jnp.int32, (size, size), 0)
    col = lax.broadcasted_iota(jnp.int32, (size, size), 1)
    x_copy.wait()
    h_real = (drawn[0] + drawn[0].T) * 0.5
    h_imag = (drawn[1] - drawn[1].T) * 0.5
    packed[...] = jnp.where(col >= row, h_real, h_imag)
    pl.semaphore_wait(barrier, expected)
    h_copy = remote(packed, packed_in, h_send, h_recv, before)
    h_copy.start()
    value[0] = h_real
    value[1] = h_imag
    for part, h in enumerate((h_real, h_imag)):
        high[0, 0, part], low[0, 0, part] = halves(h)
    h_copy.wait_recv()
    flat = packed_in[...]
    turned = flat.T
    n_real = jnp.where(col >= row, flat, turned)
    n_imag = jnp.where(row > col, flat, jnp.where(row < col, -turned, 0.0))
    x_real, x_imag = product(jnp.concatenate([n_real, n_imag], axis=0), high[0, 0], low[0, 0])
    shrink = time_step * time_step / 12.0
    m_real = shrink * (x_real - x_real.T) - 0.5 * time_step * (value[1] + n_imag)
    m_imag = -0.5 * time_step * (value[0] + n_real) - shrink * (x_imag + x_imag.T)
    for part, h in enumerate((m_real, m_imag)):
        high[0, 1, part], low[0, 1, part] = halves(h)

    def put(slot, which, first, part, value):
        rows = pl.ds(first, value.shape[0])
        high[slot, which, part, rows], low[slot, which, part, rows] = halves(value)

    u_copy = remote(unit, unit, u_send, u_recv, other)

    @pl.when(first_core)
    def _():
        eye = jnp.where(row == col, 1.0, 0.0)
        v_real = eye + m_real * 0.25
        v_imag = m_imag * 0.25
        for divisor in (3.0, 2.0, 1.0):
            v_real, v_imag = product(
                jnp.concatenate([v_real, v_imag], axis=0), high[0, 1], low[0, 1]
            )
            if divisor != 1.0:
                v_real = v_real * (1.0 / divisor)
                v_imag = v_imag * (1.0 / divisor)
            v_real = eye + v_real
        unit[:, 0] = v_real.reshape(2 * slabs, WIDTH, size)
        unit[:, 1] = v_imag.reshape(2 * slabs, WIDTH, size)
        u_copy.start()
        put(1, 1, 0, 0, v_real)
        put(1, 1, 0, 1, v_imag)

    def pair_give(part, side, j):
        slab = part * per_part + j
        return remote(
            total.at[part, side, j], got.at[0, slab], p_send.at[side, slab], p_recv.at[slab],
            device(chip + 1, side),
        )

    def total_copy(part):
        return remote(total.at[part], total.at[part], t_send.at[part], t_recv.at[part], other)

    @pl.when(second_core)
    def _():
        u_copy.wait_recv()
        for part in range(PARTS):
            span = slice(part * per_part, (part + 1) * per_part)
            sides = [unit[side * slabs + part * per_part:side * slabs + (part + 1) * per_part] for side in range(2)]
            y = stacked(jnp.concatenate(sides, axis=0))
            rows = y.shape[0] // 2
            z = y
            for divisor in (4.0, 3.0, 2.0, 1.0):
                z_real, z_imag = product(z, high[0, 1], low[0, 1])
                z = jnp.concatenate([z_real, z_imag], axis=0)
                if divisor != 1.0:
                    z = z * (1.0 / divisor)
                z = y + z
            for k in range(2):
                block = z[k * rows:(k + 1) * rows]
                total[part, :, :, k] = block.reshape(2, per_part, WIDTH, size)

            @pl.when(even)
            def _():
                for j in range(per_part):
                    for side in range(2):
                        pair_give(part, side, j).start()

            @pl.when(odd)
            def _():
                total_copy(part).start()

            for k in range(2):
                for side in range(2):
                    first = k * rows + side * (rows // 2)
                    put(1, 0, side * half + part * (rows // 2), k, z[first:first + rows // 2])

        @pl.when(odd)
        def _():
            for k in range(2):
                put(1, 1, 0, k, unit[:, k].reshape(size, size))

    @pl.when(jnp.logical_and(odd, first_core))
    def _():
        for part in range(PARTS):
            total_copy(part).wait_recv()
            for side in range(2):
                for k in range(2):
                    block = total[part, side, :, k].reshape(half // PARTS, size)
                    put(1, 0, side * half + part * (half // PARTS), k, block)

    mine = pl.multiple_of(core * half, half)
    theirs = pl.multiple_of((1 - core) * half, half)

    def give(s, j, by):
        return remote(
            keep.at[jnp.minimum(s, taken) - 1, 0, j], got.at[s, j], g_send.at[s, j], g_recv.at[s, j],
            me + 2 * by,
        )

    def share(s, j):
        return remote(keep.at[s, 0, j], swap.at[s, j], s_send.at[s, j], s_recv.at[s, j], other)

    def share_second(s):
        return remote(keep.at[s, 1], swap_second.at[s], w_send.at[s], w_recv.at[s], other)

    def finish():
        return remote(keep.at[taken - 1, core], last, f_send, f_recv, other)

    def cross(j):
        return remote(got.at[n_shifts + 1, j], crossed.at[j], c_send.at[j], c_recv.at[j], other)

    def arrived(s, j):
        sem = p_recv if s == 0 else g_recv.at[s]
        return remote(got.at[s, j], got.at[s, j], u_send, sem.at[j], other)

    def start_next(s, j):
        if s < n_shifts:
            pl.when(gives[s])(lambda: give(s + 1, j, shifts[s]).start())
        elif s == n_shifts:
            pl.when(gives_last)(lambda: give(s + 1, j, 1).start())

    for s in range(n_shifts + 1):
        slot = (s + 1) % 2

        @pl.when(takes[s])
        def _(s=s, slot=slot):
            if s > 0:
                def collect(j, _):
                    share(s - 1, j).wait_recv()
                    for k in range(2):
                        put(slot, 0, pl.multiple_of(theirs + j * WIDTH, WIDTH), k, swap[s - 1, j, k])
                    return 0

                lax.fori_loop(0, slabs, collect, 0)

            def take(j, _):
                arrived(s, j).wait_recv()
                x = got[s, j].reshape(2 * WIDTH, size)
                out = product(x, high[slot, 0], low[slot, 0])
                for k in range(2):
                    keep[s, 0, j, k] = out[k]
                start_next(s, j)
                if s < n_shifts:
                    share(s, j).start()
                    for k in range(2):
                        put(1 - slot, 0, pl.multiple_of(mine + j * WIDTH, WIDTH), k, out[k])
                return 0

            lax.fori_loop(0, slabs, take, 0)
            if s > 0:
                share_second(s - 1).wait_recv()
                for k in range(2):
                    put(slot, 1, theirs, k, swap_second[s - 1, :, k].reshape(half, size))
            out = product(stacked(got[s]), high[slot, 1], low[slot, 1])
            for k in range(2):
                keep[s, 1, :, k] = out[k].reshape(slabs, WIDTH, size)
            if s < n_shifts:
                share_second(s).start()
                for k in range(2):
                    put(1 - slot, 1, mine, k, out[k])

        if s > 0:
            @pl.when(jnp.logical_and(odd, jnp.logical_not(takes[s])))
            def _(s=s):
                if s > 0:
                    @pl.when(takes[s - 1])
                    def _():
                        def skip(j, _):
                            share(s - 1, j).wait_recv()
                            return 0

                        lax.fori_loop(0, slabs, skip, 0)
                        share_second(s - 1).wait_recv()

                def send(j, _):
                    start_next(s, j)
                    return 0

                lax.fori_loop(0, slabs, send, 0)

    def into_value(first, k, block):
        value[k, pl.ds(first, block.shape[0])] = block

    @pl.when(odd)
    def _():
        finish().start()
        for k in range(2):
            into_value(mine, k, keep[taken - 1, 1 - core, :, k].reshape(half, size))
        finish().wait_recv()
        for k in range(2):
            into_value(theirs, k, last[:, k].reshape(half, size))

    @pl.when(takes_last)
    def _():
        s = n_shifts + 1
        left_high, left_low = high.at[1, 1 - core], low.at[1, 1 - core]

        def take(j, _):
            arrived(s, j).wait_recv()
            cross(j).start()
            out = product(got[s, j].reshape(2 * WIDTH, size), left_high, left_low)
            for k in range(2):
                into_value(pl.multiple_of(mine + j * WIDTH, WIDTH), k, out[k])
            return 0

        lax.fori_loop(0, slabs, take, 0)
        for part in range(PARTS):
            for j in range(part * per_part, (part + 1) * per_part):
                cross(j).wait_recv()
            out = product(stacked(crossed[part * per_part:(part + 1) * per_part]), left_high, left_low)
            for k in range(2):
                into_value(pl.multiple_of(theirs + part * per_part * WIDTH, WIDTH), k, out[k])

    @pl.when(jnp.logical_and(chip == 0, first_core))
    def _():
        for k in range(2):
            into_value(0, k, unit[:, k].reshape(size, size))

    @pl.when(jnp.logical_and(chip == 0, second_core))
    def _():
        for part in range(PARTS):
            for side in range(2):
                for k in range(2):
                    block = total[part, side, :, k].reshape(half // PARTS, size)
                    into_value(side * half + part * (half // PARTS), k, block)

    o_ref[0] = value[0].T
    o_ref[1] = value[1].T

    h_copy.wait_send()
    pl.when(first_core)(lambda: u_copy.wait_send())

    @pl.when(jnp.logical_and(even, second_core))
    def _():
        for part in range(PARTS):
            for j in range(per_part):
                for side in range(2):
                    pair_give(part, side, j).wait_send()

    @pl.when(jnp.logical_and(odd, second_core))
    def _():
        for part in range(PARTS):
            total_copy(part).wait_send()

    @pl.when(odd)
    def _():
        def drain(j, _):
            for s in range(n_shifts):
                pl.when(gives[s])(lambda s=s: give(s + 1, j, shifts[s]).wait_send())
                pl.when(takes[s])(lambda s=s: share(s, j).wait_send())
            pl.when(gives_last)(lambda: give(n_shifts + 1, j, 1).wait_send())
            return 0

        lax.fori_loop(0, slabs, drain, 0)
        for s in range(n_shifts):
            pl.when(takes[s])(lambda s=s: share_second(s).wait_send())
        finish().wait_send()

    @pl.when(takes_last)
    def _():
        def drain(j, _):
            cross(j).wait_send()
            return 0

        lax.fori_loop(0, slabs, drain, 0)


def on_device(samples):
    x = samples[0]
    size = x.shape[-1]
    devices = lax.axis_size("tm")
    steps = (devices // 2).bit_length() - 1
    slabs = size // 2 // WIDTH
    f32, bf16 = jnp.float32, jnp.bfloat16
    slab = (2, WIDTH, size)
    dma = pltpu.SemaphoreType.DMA
    out = pl.pallas_call(
        functools.partial(kernel, devices),
        out_shape=jax.ShapeDtypeStruct(x.shape, f32),
        in_specs=[pl.BlockSpec(memory_space=pltpu.HBM)],
        out_specs=pl.BlockSpec(memory_space=pltpu.VMEM),
        scratch_shapes=[
            pltpu.VMEM((2, size, size), f32),
            pltpu.VMEM((size, size), f32),
            pltpu.VMEM((size, size), f32),
            pltpu.VMEM((2, size, size), f32),
            pltpu.VMEM((2 * slabs, *slab), f32),
            pltpu.VMEM((PARTS, 2, slabs // PARTS, *slab), f32),
            pltpu.VMEM((steps, 2, slabs, *slab), f32),
            pltpu.VMEM((steps + 1, slabs, *slab), f32),
            pltpu.VMEM((steps, slabs, *slab), f32),
            pltpu.VMEM((steps, slabs, *slab), f32),
            pltpu.VMEM((slabs, *slab), f32),
            pltpu.VMEM((slabs, *slab), f32),
            pltpu.VMEM((2, 2, 2, size, size), bf16),
            pltpu.VMEM((2, 2, 2, size, size), bf16),
            dma, dma, dma, dma, dma, dma((PARTS,)), dma((PARTS,)),
            dma((2, slabs)), dma((slabs,)),
            dma((steps + 1, slabs)), dma((steps + 1, slabs)),
            dma((steps, slabs)), dma((steps, slabs)),
            dma((steps,)), dma((steps,)),
            dma, dma, dma((slabs,)), dma((slabs,)),
        ],
        compiler_params=pltpu.CompilerParams(
            collective_id=0, has_side_effects=True, vmem_limit_bytes=48 << 20
        ),
        name="propagators",
    )(x)
    return out[None]


def solution(mesh):
    spec = P("tm", None, None, None)
    return jax.shard_map(on_device, mesh=mesh, in_specs=(spec,), out_specs=spec, check_vma=False)
```

time: 84.4 us -> 78 us (0.924)
  the two profiles are of different devices: /device:TPU:61 before, /device:TPU:21 now
where the time goes in v2:
time: 78 us; the launch traced here: 77.9 us
  Pallas kernels  76 us (97%)
  local copies, waits for them, and re-layouts  1.84 us (2%)
    pallas_call x1, Pallas kernels, on_device(): pl.pallas_call(functools.partial(kernel, devices), out_shape=jax.ShapeDty...  76 us
    unnamed x3, local copies, waits for them, and re-layouts  1.84 us

profile of v2, /device:TPU:21, one launch (start us, length us, event | category | flops | bytes accessed | tf_op | source)
XLA Modules:
  0.0 77.9 jit_solution(13949927693246807814)
XLA Ops:
  0.0 0.0 copy-start
  0.0 1.0 %copy-done = f32[1,2,256,256]{3,2,1,0:T(8,128)S(1)} copy-done((f32[1,2,256,256]{3,2,1,0:T(8,128)S(1)}, f32[1,2,256,256]{3,2,1,0:T(8,128)}, u32[]{:S(2)}) %copy-start) | copy-done | bytes 524312
  1.0 76.0 %propagators.1 = f32[2,256,256]{2,1,0:T(8,128)S(1)} custom-call(f32[2,256,256]{2,1,0:T(8,128)S(1)} %bitcast.3), custom_call_target="tpu_custom_call" | custom-call | tf_op jit(solution)/shard_map/propagators/pallas_call | solution.py:402
  77.1 0.8 %copy.3 = f32[1,2,256,256]{3,2,1,0:T(8,128)} copy(f32[1,2,256,256]{3,2,1,0:T(8,128)S(1)} %bitcast.2) | data formatting | bytes 1048576
Async XLA Ops:
  0.0 1.0 %copy-start = (f32[1,2,256,256]{3,2,1,0:T(8,128)S(1)}, f32[1,2,256,256]{3,2,1,0:T(8,128)}, u32[]{:S(2)}) copy-start(f32[1,2,256,256]{3,2,1,0:T(8,128)} %param.1) | copy-start | bytes 1572868

commit v3 on v2

--- a/solution.py
+++ b/solution.py
@@ -168,11 +168,7 @@
     @pl.when(second_core)
     def _():
         u_copy.wait_recv()
-        for part in range(PARTS):
-            span = slice(part * per_part, (part + 1) * per_part)
-            sides = [unit[side * slabs + part * per_part:side * slabs + (part + 1) * per_part] for side in range(2)]
-            y = stacked(jnp.concatenate(sides, axis=0))
-            rows = y.shape[0] // 2
+        def applied(y):
             z = y
             for divisor in (4.0, 3.0, 2.0, 1.0):
                 z_real, z_imag = product(z, high[0, 1], low[0, 1])
@@ -180,24 +176,40 @@
                 if divisor != 1.0:
                     z = z * (1.0 / divisor)
                 z = y + z
-            for k in range(2):
-                block = z[k * rows:(k + 1) * rows]
-                total[part, :, :, k] = block.reshape(2, per_part, WIDTH, size)
-
-            @pl.when(even)
-            def _():
+            return z
+
+        @pl.when(odd)
+        def _():
+            z = applied(stacked(unit[...]))
+            for k in range(2):
+                block = z[k * size:(k + 1) * size].reshape(2, PARTS, per_part, WIDTH, size)
+                for part in range(PARTS):
+                    total[part, :, :, k] = block[:, part]
+            for part in range(PARTS):
+                total_copy(part).start()
+            for k in range(2):
+                put(1, 0, 0, k, z[k * size:(k + 1) * size])
+
+        @pl.when(even)
+        def _():
+            for part in range(PARTS):
+                sides = [
+                    unit[side * slabs + part * per_part:side * slabs + (part + 1) * per_part]
+                    for side in range(2)
+                ]
+                y = stacked(jnp.concatenate(sides, axis=0))
+                rows = y.shape[0] // 2
+                z = applied(y)
+                for k in range(2):
+                    block = z[k * rows:(k + 1) * rows]
+                    total[part, :, :, k] = block.reshape(2, per_part, WIDTH, size)
                 for j in range(per_part):
                     for side in range(2):
                         pair_give(part, side, j).start()
-
-            @pl.when(odd)
-            def _():
-                total_copy(part).start()
-
-            for k in range(2):
-                for side in range(2):
-                    first = k * rows + side * (rows // 2)
-                    put(1, 0, side * half + part * (rows // 2), k, z[first:first + rows // 2])
+                for k in range(2):
+                    for side in range(2):
+                        first = k * rows + side * (rows // 2)
+                        put(1, 0, side * half + part * (rows // 2), k, z[first:first + rows // 2])
 
         @pl.when(odd)
         def _():

time: 78 us -> 77.4 us (level)
  no operation moved by 1% of the time
where the time goes in v3:
time: 77.4 us; the launch traced here: 77.3 us
  Pallas kernels  75.4 us (97%)
  local copies, waits for them, and re-layouts  1.84 us (2%)
    pallas_call x1, Pallas kernels, on_device(): pl.pallas_call(functools.partial(kernel, devices), out_shape=jax.ShapeDty...  75.4 us
    unnamed x3, local copies, waits for them, and re-layouts  1.84 us

profile of v3, /device:TPU:21, one launch (start us, length us, event | category | flops | bytes accessed | tf_op | source)
XLA Modules:
  0.0 77.3 jit_solution(5234745181082272808)
XLA Ops:
  0.0 0.0 copy-start
  0.0 1.0 %copy-done = f32[1,2,256,256]{3,2,1,0:T(8,128)S(1)} copy-done((f32[1,2,256,256]{3,2,1,0:T(8,128)S(1)}, f32[1,2,256,256]{3,2,1,0:T(8,128)}, u32[]{:S(2)}) %copy-start) | copy-done | bytes 524312
  1.0 75.4 %propagators.1 = f32[2,256,256]{2,1,0:T(8,128)S(1)} custom-call(f32[2,256,256]{2,1,0:T(8,128)S(1)} %bitcast.3), custom_call_target="tpu_custom_call" | custom-call | tf_op jit(solution)/shard_map/propagators/pallas_call | solution.py:414
  76.5 0.8 %copy.3 = f32[1,2,256,256]{3,2,1,0:T(8,128)} copy(f32[1,2,256,256]{3,2,1,0:T(8,128)S(1)} %bitcast.2) | data formatting | bytes 1048576
Async XLA Ops:
  0.0 1.0 %copy-start = (f32[1,2,256,256]{3,2,1,0:T(8,128)S(1)}, f32[1,2,256,256]{3,2,1,0:T(8,128)}, u32[]{:S(2)}) copy-start(f32[1,2,256,256]{3,2,1,0:T(8,128)} %param.1) | copy-start | bytes 1572868

commit v4 on v2

--- a/solution.py
+++ b/solution.py
@@ -41,9 +41,9 @@
 
 def kernel(
     devices, x_ref, o_ref,
-    drawn, packed, packed_in, value, unit, total, keep, got, swap, swap_second, last, crossed, high, low,
+    drawn, packed, packed_in, value, unit, total, keep, got, swap, swap_second, last, high, low,
     x_sem, h_send, h_recv, u_send, u_recv, t_send, t_recv, p_send, p_recv, g_send, g_recv,
-    s_send, s_recv, w_send, w_recv, f_send, f_recv, c_send, c_recv,
+    s_send, s_recv, w_send, w_recv, f_send, f_recv,
 ):
     size = x_ref.shape[-1]
     half = size // 2
@@ -53,8 +53,6 @@
     me = lax.axis_index("tm")
     core = lax.rem(me, 2)
     chip = me // 2
-    odd = lax.rem(chip, 2) == 1
-    even = jnp.logical_not(odd)
     first_core = core == 0
     second_core = core == 1
     other = me + 1 - 2 * core
@@ -70,11 +68,10 @@
         shifts.append(shift)
         shift *= 2
     n_shifts = len(shifts)
-    takes = [odd] + [jnp.logical_and(odd, chip > by) for by in shifts]
-    gives = [jnp.logical_and(odd, chip + by < chips) for by in shifts]
-    gives_last = jnp.logical_and(odd, chip + 1 < chips)
-    takes_last = jnp.logical_and(even, chip > 0)
-    taken = sum(t.astype(jnp.int32) for t in takes)
+    takes = [chip >= by for by in [1] + shifts]
+    gives_first = chip + 1 < chips
+    gives = [chip + by < chips for by in shifts]
+    taken = jnp.maximum(sum(t.astype(jnp.int32) for t in takes), 1)
 
     barrier = pltpu.get_barrier_semaphore()
     expected = 0
@@ -88,11 +85,10 @@
 
     always = chip >= 0
     pairs = [(always, other), (always, before), (always, after)]
-    pairs += [(jnp.logical_and(even, second_core), device(chip + 1, c)) for c in range(2)]
-    pairs += [(odd, device(chip - 1, 1))]
+    pairs += [(jnp.logical_and(gives_first, second_core), device(chip + 1, c)) for c in range(2)]
+    pairs += [(takes[0], device(chip - 1, 1))]
     for by, t, g in zip(shifts, takes[1:], gives):
         pairs += [(t, me - 2 * by), (g, me + 2 * by)]
-    pairs += [(gives_last, me + 2), (takes_last, me - 2)]
     for when, where in pairs:
         expected = expected + greet(when, where)
 
@@ -168,11 +164,7 @@
     @pl.when(second_core)
     def _():
         u_copy.wait_recv()
-        for part in range(PARTS):
-            span = slice(part * per_part, (part + 1) * per_part)
-            sides = [unit[side * slabs + part * per_part:side * slabs + (part + 1) * per_part] for side in range(2)]
-            y = stacked(jnp.concatenate(sides, axis=0))
-            rows = y.shape[0] // 2
+        def applied(y):
             z = y
             for divisor in (4.0, 3.0, 2.0, 1.0):
                 z_real, z_imag = product(z, high[0, 1], low[0, 1])
@@ -180,31 +172,35 @@
                 if divisor != 1.0:
                     z = z * (1.0 / divisor)
                 z = y + z
+            return z
+
+        for part in range(PARTS):
+            sides = [
+                unit[side * slabs + part * per_part:side * slabs + (part + 1) * per_part]
+                for side in range(2)
+            ]
+            y = stacked(jnp.concatenate(sides, axis=0))
+            rows = y.shape[0] // 2
+            z = applied(y)
             for k in range(2):
                 block = z[k * rows:(k + 1) * rows]
                 total[part, :, :, k] = block.reshape(2, per_part, WIDTH, size)
-
-            @pl.when(even)
-            def _():
+            @pl.when(gives_first)
+            def _(part=part):
                 for j in range(per_part):
                     for side in range(2):
                         pair_give(part, side, j).start()
 
-            @pl.when(odd)
-            def _():
-                total_copy(part).start()
-
+            total_copy(part).start()
             for k in range(2):
                 for side in range(2):
                     first = k * rows + side * (rows // 2)
                     put(1, 0, side * half + part * (rows // 2), k, z[first:first + rows // 2])
 
-        @pl.when(odd)
-        def _():
-            for k in range(2):
-                put(1, 1, 0, k, unit[:, k].reshape(size, size))
-
-    @pl.when(jnp.logical_and(odd, first_core))
+        for k in range(2):
+            put(1, 1, 0, k, unit[:, k].reshape(size, size))
+
+    @pl.when(first_core)
     def _():
         for part in range(PARTS):
             total_copy(part).wait_recv()
@@ -231,9 +227,6 @@
     def finish():
         return remote(keep.at[taken - 1, core], last, f_send, f_recv, other)
 
-    def cross(j):
-        return remote(got.at[n_shifts + 1, j], crossed.at[j], c_send.at[j], c_recv.at[j], other)
-
     def arrived(s, j):
         sem = p_recv if s == 0 else g_recv.at[s]
         return remote(got.at[s, j], got.at[s, j], u_send, sem.at[j], other)
@@ -241,8 +234,6 @@
     def start_next(s, j):
         if s < n_shifts:
             pl.when(gives[s])(lambda: give(s + 1, j, shifts[s]).start())
-        elif s == n_shifts:
-            pl.when(gives_last)(lambda: give(s + 1, j, 1).start())
 
     for s in range(n_shifts + 1):
         slot = (s + 1) % 2
@@ -284,70 +275,39 @@
                 for k in range(2):
                     put(1 - slot, 1, mine, k, out[k])
 
-        if s > 0:
-            @pl.when(jnp.logical_and(odd, jnp.logical_not(takes[s])))
-            def _(s=s):
-                if s > 0:
-                    @pl.when(takes[s - 1])
-                    def _():
-                        def skip(j, _):
-                            share(s - 1, j).wait_recv()
-                            return 0
-
-                        lax.fori_loop(0, slabs, skip, 0)
-                        share_second(s - 1).wait_recv()
-
-                def send(j, _):
-                    start_next(s, j)
-                    return 0
-
-                lax.fori_loop(0, slabs, send, 0)
+        @pl.when(jnp.logical_not(takes[s]))
+        def _(s=s):
+            if s > 0:
+                @pl.when(takes[s - 1])
+                def _():
+                    def skip(j, _):
+                        share(s - 1, j).wait_recv()
+                        return 0
+
+                    lax.fori_loop(0, slabs, skip, 0)
+                    share_second(s - 1).wait_recv()
+
+            if s == 0:
+                for part in range(PARTS):
+                    span = slice(part * per_part, (part + 1) * per_part)
+                    keep[0, 0, span] = total[part, core]
+                keep[0, 1] = unit[pl.ds(core * slabs, slabs)]
+
+            def send(j, _):
+                start_next(s, j)
+                return 0
+
+            lax.fori_loop(0, slabs, send, 0)
 
     def into_value(first, k, block):
         value[k, pl.ds(first, block.shape[0])] = block
 
-    @pl.when(odd)
-    def _():
-        finish().start()
-        for k in range(2):
-            into_value(mine, k, keep[taken - 1, 1 - core, :, k].reshape(half, size))
-        finish().wait_recv()
-        for k in range(2):
-            into_value(theirs, k, last[:, k].reshape(half, size))
-
-    @pl.when(takes_last)
-    def _():
-        s = n_shifts + 1
-        left_high, left_low = high.at[1, 1 - core], low.at[1, 1 - core]
-
-        def take(j, _):
-            arrived(s, j).wait_recv()
-            cross(j).start()
-            out = product(got[s, j].reshape(2 * WIDTH, size), left_high, left_low)
-            for k in range(2):
-                into_value(pl.multiple_of(mine + j * WIDTH, WIDTH), k, out[k])
-            return 0
-
-        lax.fori_loop(0, slabs, take, 0)
-        for part in range(PARTS):
-            for j in range(part * per_part, (part + 1) * per_part):
-                cross(j).wait_recv()
-            out = product(stacked(crossed[part * per_part:(part + 1) * per_part]), left_high, left_low)
-            for k in range(2):
-                into_value(pl.multiple_of(theirs + part * per_part * WIDTH, WIDTH), k, out[k])
-
-    @pl.when(jnp.logical_and(chip == 0, first_core))
-    def _():
-        for k in range(2):
-            into_value(0, k, unit[:, k].reshape(size, size))
-
-    @pl.when(jnp.logical_and(chip == 0, second_core))
-    def _():
-        for part in range(PARTS):
-            for side in range(2):
-                for k in range(2):
-                    block = total[part, side, :, k].reshape(half // PARTS, size)
-                    into_value(side * half + part * (half // PARTS), k, block)
+    finish().start()
+    for k in range(2):
+        into_value(mine, k, keep[taken - 1, 1 - core, :, k].reshape(half, size))
+    finish().wait_recv()
+    for k in range(2):
+        into_value(theirs, k, last[:, k].reshape(half, size))
 
     o_ref[0] = value[0].T
     o_ref[1] = value[1].T
@@ -355,39 +315,30 @@
     h_copy.wait_send()
     pl.when(first_core)(lambda: u_copy.wait_send())
 
-    @pl.when(jnp.logical_and(even, second_core))
+    @pl.when(jnp.logical_and(gives_first, second_core))
     def _():
         for part in range(PARTS):
             for j in range(per_part):
                 for side in range(2):
                     pair_give(part, side, j).wait_send()
 
-    @pl.when(jnp.logical_and(odd, second_core))
+    @pl.when(second_core)
     def _():
         for part in range(PARTS):
             total_copy(part).wait_send()
 
-    @pl.when(odd)
+    @pl.when(always)
     def _():
         def drain(j, _):
             for s in range(n_shifts):
                 pl.when(gives[s])(lambda s=s: give(s + 1, j, shifts[s]).wait_send())
                 pl.when(takes[s])(lambda s=s: share(s, j).wait_send())
-            pl.when(gives_last)(lambda: give(n_shifts + 1, j, 1).wait_send())
             return 0
 
         lax.fori_loop(0, slabs, drain, 0)
         for s in range(n_shifts):
             pl.when(takes[s])(lambda s=s: share_second(s).wait_send())
         finish().wait_send()
-
-    @pl.when(takes_last)
-    def _():
-        def drain(j, _):
-            cross(j).wait_send()
-            return 0
-
-        lax.fori_loop(0, slabs, drain, 0)
 
 
 def on_device(samples):
@@ -416,7 +367,6 @@
             pltpu.VMEM((steps, slabs, *slab), f32),
             pltpu.VMEM((steps, slabs, *slab), f32),
             pltpu.VMEM((slabs, *slab), f32),
-            pltpu.VMEM((slabs, *slab), f32),
             pltpu.VMEM((2, 2, 2, size, size), bf16),
             pltpu.VMEM((2, 2, 2, size, size), bf16),
             dma, dma, dma, dma, dma, dma((PARTS,)), dma((PARTS,)),
@@ -424,7 +374,7 @@
             dma((steps + 1, slabs)), dma((steps + 1, slabs)),
             dma((steps, slabs)), dma((steps, slabs)),
             dma((steps,)), dma((steps,)),
-            dma, dma, dma((slabs,)), dma((slabs,)),
+            dma, dma,
         ],
         compiler_params=pltpu.CompilerParams(
             collective_id=0, has_side_effects=True, vmem_limit_bytes=48 << 20

time: 78 us -> 80.2 us (1.028)
  the two profiles are of different devices: /device:TPU:21 before, /device:TPU:52 now
where the time goes in v4:
time: 80.2 us; the launch traced here: 80.1 us
  Pallas kernels  78.2 us (98%)
  local copies, waits for them, and re-layouts  1.84 us (2%)
    pallas_call x1, Pallas kernels, on_device(): pl.pallas_call(functools.partial(kernel, devices), out_shape=jax.ShapeDty...  78.2 us
    unnamed x3, local copies, waits for them, and re-layouts  1.84 us

profile of v4, /device:TPU:52, one launch (start us, length us, event | category | flops | bytes accessed | tf_op | source)
XLA Modules:
  0.0 80.1 jit_solution(2759124164179824431)
XLA Ops:
  0.0 0.0 copy-start
  0.0 1.0 %copy-done = f32[1,2,256,256]{3,2,1,0:T(8,128)S(1)} copy-done((f32[1,2,256,256]{3,2,1,0:T(8,128)S(1)}, f32[1,2,256,256]{3,2,1,0:T(8,128)}, u32[]{:S(2)}) %copy-start) | copy-done | bytes 524312
  1.0 78.2 %propagators.1 = f32[2,256,256]{2,1,0:T(8,128)S(1)} custom-call(f32[2,256,256]{2,1,0:T(8,128)S(1)} %bitcast.3), custom_call_target="tpu_custom_call" | custom-call | tf_op jit(solution)/shard_map/propagators/pallas_call | solution.py:353
  79.3 0.8 copy.3
Async XLA Ops:
  0.0 1.0 %copy-start = (f32[1,2,256,256]{3,2,1,0:T(8,128)S(1)}, f32[1,2,256,256]{3,2,1,0:T(8,128)}, u32[]{:S(2)}) copy-start(f32[1,2,256,256]{3,2,1,0:T(8,128)} %param.1) | copy-start | bytes 1572868
